TPU v7x, 32 devices: a whole 2x2x4 slice. The times are simulated.
32 devices in a mesh: dp: 4 (over z), seq: 8 (over y, x, core).
Axes of the slice: x: 2, y: 2, z: 4, core: 2. Of those that a mesh axis runs over, the one named last changes fastest.
Arguments:
- q_video: bfloat16 [12288, 2048], P(('dp', 'seq')), parts along dimension 0, may hold values from -5 to 5
- k_video: bfloat16 [12288, 2048], P(('dp', 'seq')), parts along dimension 0, may hold values from -5 to 5
- v_video: bfloat16 [12288, 2048], P(('dp', 'seq')), parts along dimension 0, may hold values from -6 to 6
- q_audio: bfloat16 [1024, 2048], P(('dp', 'seq')), parts along dimension 0, may hold values from -5 to 5
- k_audio: bfloat16 [1024, 2048], P(('dp', 'seq')), parts along dimension 0, may hold values from -5 to 5
- v_audio: bfloat16 [1024, 2048], P(('dp', 'seq')), parts along dimension 0, may hold values from -6 to 6
Outputs:
- video_out: bfloat16 [12288, 2048], P(('dp', 'seq')), parts along dimension 0
- audio_out: bfloat16 [1024, 2048], P(('dp', 'seq')), parts along dimension 0
There are 4 independent parts, one for each index of `dp`. A program takes and returns all parts, laid end to end along the dimension named above; each array names one. Nothing has to cross between parts.
All inputs are finite; a program needn't handle non-finite values.
Results may differ from a plain program's by a relative error of at most 0.0049.
Values may be sent and summed in bfloat16 or wider, within the bound.
A program may use at most 128 MiB of HBM per device.

v0:
```python
import jax
import jax.numpy as jnp
from jax import lax
from jax.sharding import PartitionSpec as P

H = 16


def head_major(matrix, head_count):
    return matrix.reshape(matrix.shape[0], head_count, -1).transpose(1, 0, 2)


def settle(mixed):
    return mixed * lax.rsqrt(jnp.mean(mixed * mixed, axis=-1, keepdims=True) + 1e-06)


def video_head(triple):
    queries, key_rows, value_rows = triple
    factor = queries.shape[-1] ** (-0.5)
    scores = jnp.dot(queries, key_rows.T, preferred_element_type=jnp.float32) * factor
    row_peak = jnp.max(scores, axis=-1, keepdims=True)
    exponent = jnp.exp(scores - row_peak)
    weights = (exponent / jnp.sum(exponent, axis=-1, keepdims=True)).astype(jnp.bfloat16)
    return settle(jnp.dot(weights, value_rows, preferred_element_type=jnp.float32))


def audio_partial(triple):
    queries, key_rows, value_rows = triple
    factor = queries.shape[-1] ** (-0.5)
    scores = jnp.dot(queries, key_rows.T, preferred_element_type=jnp.float32) * factor
    block_peak = jnp.max(scores, axis=-1)
    exponent = jnp.exp(scores - block_peak[:, None])
    totals = jnp.sum(exponent, axis=-1)
    numerators = jnp.dot(
        exponent.astype(jnp.bfloat16), value_rows, preferred_element_type=jnp.float32
    )
    return (numerators, block_peak, totals)


def local(q_video, k_video, v_video, q_audio, k_audio, v_audio):
    all_queries, all_keys, all_values = (
        lax.all_gather(q_audio, "seq", axis=0, tiled=True),
        lax.all_gather(k_audio, "seq", axis=0, tiled=True),
        lax.all_gather(v_audio, "seq", axis=0, tiled=True),
    )
    video_rows = lax.map(
        video_head, (head_major(q_video, H), head_major(all_keys, H), head_major(all_values, H))
    )
    video_out = video_rows.transpose(1, 0, 2).reshape(q_video.shape[0], -1).astype(jnp.bfloat16)
    numerators, block_peak, totals = lax.map(
        audio_partial, (head_major(all_queries, H), head_major(k_video, H), head_major(v_video, H))
    )
    overall = lax.pmax(block_peak.astype(jnp.bfloat16), "seq").astype(block_peak.dtype)
    weight = jnp.exp(block_peak - overall)
    summed, denominator = (
        lax.psum_scatter(numerators * weight[..., None], "seq", scatter_dimension=1, tiled=True),
        lax.psum_scatter(totals * weight, "seq", scatter_dimension=1, tiled=True),
    )
    audio_mix = settle(summed / denominator[..., None])
    audio_out = audio_mix.transpose(1, 0, 2).reshape(audio_mix.shape[1], -1).astype(jnp.bfloat16)
    return (video_out, audio_out)


def solution(mesh):
    return jax.shard_map(
        local,
        mesh=mesh,
        in_specs=(
            P(("dp", "seq"), None),
            P(("dp", "seq"), None),
            P(("dp", "seq"), None),
            P(("dp", "seq"), None),
            P(("dp", "seq"), None),
            P(("dp", "seq"), None),
        ),
        out_specs=(P(("dp", "seq"), None), P(("dp", "seq"), None)),
        check_vma=False,
    )
```

profile of v0, /device:TPU:0, one launch (start us, length us, event | category | flops | bytes accessed | tf_op | source)
XLA Modules:
  0.0 180.9 jit_solution(15698158150450828108)
XLA Ops:
  9.5 2.7 %copy.32 = bf16[384,2048]{0,1:T(8,128)(2,1)} copy(bf16[384,2048]{1,0:T(8,128)(2,1)} %param.11) | data formatting | bytes 3145728 | tf_op args[1]
  13.0 1.9 %copy.24 = bf16[384,2048]{0,1:T(8,128)(2,1)S(1)} copy(bf16[384,2048]{1,0:T(8,128)(2,1)} %param.10) | data formatting | bytes 3145728 | tf_op args[0]
  14.9 21.2 %all-gather.8.cloned.1.call-done = bf16[256,2048]{1,0:T(8,128)(2,1)} async-done(((bf16[32,2048]{1,0:T(8,128)(2,1)}), bf16[256,2048]{1,0:T(8,128)(2,1)}) %all-gather.8.cloned.1.call-update) | async-done | bytes 1048592 | tf_op jit(solution)/shard_map/all_gather | solution.py:42
  36.1 2.3 %copy.31 = bf16[256,2048]{0,1:T(8,128)(2,1)} copy(bf16[256,2048]{1,0:T(8,128)(2,1)} %all-gather.8.cloned.1.call-done) | data formatting | bytes 2097152 | tf_op jit(solution)/shard_map/all_gather | solution.py:42
  38.4 40.3 %while.25 = (s32[]{:T(128)}, f32[16,256,128]{2,1,0:T(8,128)}, f32[16,256]{1,0:T(8,128)S(1)}, f32[16,256]{1,0:T(8,128)S(1)}, bf16[16,256,128]{1,2,0:T(8,128)(2,1)...) while((s32[]{:T(128)}, f32[16,256,128]{2,1,0:T(8,128)}, ...), condition=%wide.region_8.9_spmd, body=%wide.region_5.8_spmd.sunk | while | flops 50920960 | bytes 1583205 | solution.py:50
  40.9 1.3 fusion.39
  43.4 1.3 fusion.39
  46.0 1.3 fusion.39
  48.5 1.3 fusion.39
  53.5 1.3 fusion.39
  58.6 1.3 fusion.39
  63.6 1.3 fusion.39
  66.1 1.3 fusion.39
  71.2 1.3 fusion.39
  73.7 1.3 fusion.39
  76.2 1.3 fusion.39
  78.7 13.6 %pmax.7 = bf16[16,256]{1,0:T(8,128)(2,1)S(1)} all-reduce(bf16[16,256]{1,0:T(8,128)(2,1)S(1)} %convert_element_type.33), channel_id=1, replica_groups=mesh['dp'=4,'seq'=8] {'seq'}, use_global_device_ids=true, to_apply=%region_9.10 | all-reduce | flops 4096 | bytes 16384 | tf_op jit(solution)/shard_map/pmax | solution.py:53
  93.2 3.5 %broadcast_multiply_fusion = f32[16,256,128]{2,1,0:T(8,128)} fusion(f32[16,256,128]{2,1,0:T(8,128)} %get-tuple-element.69, f32[16,256]{1,0:T(8,128)S(1)} %get-tuple-element.121), kind=kLoop, calls=%fused_computation.31 | loop fusion | flops 524288 | bytes 4210688 | tf_op jit(solution)/shard_map/mul | solution.py:56
  96.8 1.5 copy.25
  98.3 2.3 %copy.26 = bf16[256,2048]{0,1:T(8,128)(2,1)} copy(bf16[256,2048]{1,0:T(8,128)(2,1)} %all-gather.6.cloned.1.call-done) | data formatting | bytes 2097152 | tf_op jit(solution)/shard_map/all_gather | solution.py:44
  100.6 33.8 %while.24 = (s32[]{:T(128)}, bf16[16,384,128]{1,2,0:T(8,128)(2,1)}, bf16[16,384,128]{1,2,0:T(8,128)(2,1)S(1)}, bf16[16,256,128]{1,2,0:T(8,128)(2,1)S(1)}, bf16[16,256,128]{1,2,0:T(8,128)(2,1)}, /*index=5*/s32[]{:T(128)}) while((s32[]{:T(128)}, bf16[16,384,128]{1,2,0:T(8,128)(2,1)}, bf16[16,384,128]{1,2,0:T(8,128)(2,1)S(1)}, ...), condition=%wide.region_4.5_spmd, body=%wide.region_0.4_spmd.sunk | while | flops 51166848 | bytes 2014789 | solution.py:46
  134.4 2.7 %copy.38 = bf16[384,2048]{1,0:T(8,128)(2,1)} copy(bf16[384,2048]{0,1:T(8,128)(2,1)} %bitcast.17) | data formatting | bytes 3145728 | tf_op jit(solution)/shard_map/convert_element_type | solution.py:49
  137.8 33.5 %reduce-scatter.5.cloned.1.call-done = f32[16,32,128]{2,1,0:T(8,128)} async-done(((f32[16,256,128]{2,1,0:T(8,128)}), f32[16,32,128]{2,1,0:T(8,128)}) %reduce-scatter.5.cloned.1.call-update) | async-done | bytes 262160 | tf_op jit(solution)/shard_map/reduce_scatter | solution.py:56
  172.6 1.8 %copy_bitcast_fusion = bf16[32,2048]{1,0:T(8,128)(2,1)} fusion(f32[16,32]{1,0:T(8,128)S(1)} %add_rsqrt_fusion.1, f32[16,32,128]{2,1,0:T(8,128)} %reduce-scatter.5.cloned.1.call-done, f32[16,32]{1,0:T(8,128)S(1)} %copy.40), kind=kLoop, calls=%fused_computation.35 | loop fusion | flops 196608 | bytes 397312 | tf_op jit(solution)/shard_map/convert_element_type | solution.py:60
  (175 shorter events, 65.4 us)
Async XLA Ops:
  7.2 28.9 %all-gather.8.cloned.1.call-start = ((), (), s32[]{:S(2)}) async-start(), calls=%async_computation.4 | async-start | bytes 1179648 | tf_op jit(solution)/shard_map/all_gather | solution.py:42
  7.9 88.9 %all-gather.4.cloned.1.call-start = ((), (), s32[]{:S(2)}) async-start(), calls=%async_computation.2 | async-start | bytes 1179648 | tf_op jit(solution)/shard_map/all_gather | solution.py:43
  8.6 89.7 %all-gather.6.cloned.1.call-start = ((), (), s32[]{:S(2)}) async-start(), calls=%async_computation.3 | async-start | bytes 1179648 | tf_op jit(solution)/shard_map/all_gather | solution.py:44
  9.4 127.6 %reduce-scatter.7.cloned.1.call-start = ((), (), s32[]{:S(2)}) async-start(), calls=%async_computation.6 | async-start | bytes 147456
  9.5 2.7 %copy-start = (bf16[384,2048]{1,0:T(8,128)(2,1)S(1)}, bf16[384,2048]{1,0:T(8,128)(2,1)}, u32[]{:S(2)}) copy-start(bf16[384,2048]{1,0:T(8,128)(2,1)} %param.12) | copy-start | bytes 4718596
  93.1 78.2 %reduce-scatter.5.cloned.1.call-start = ((), (), s32[]{:S(2)}) async-start(), calls=%async_computation.5 | async-start | bytes 2359296 | tf_op jit(solution)/shard_map/reduce_scatter | solution.py:56
Sparse Core Ops, SparseCore 0:
  9.9 26.1 all-gather.7
  38.0 23.5 all-gather.3
  63.5 23.6 all-gather.5
  93.3 33.2 reduce-scatter.6
  130.1 41.2 reduce-scatter.4
where the time goes:
time: 183 us; the launch traced here: 181 us
  waiting for transfers between devices  56.9 us (31%)
  matrix products  56.7 us (31%)
  other arithmetic  21.9 us (12%)
  local copies, waits for them, and re-layouts  17 us (9%)
  between operations  13.9 us (8%)
  blocking collectives  13.6 us (7%)
    reduce_scatter x1, waiting for transfers between devices, local(): lax.psum_scatter(numerators * weight[..., None], 'seq', scatter_dimension...  33.5 us
    all_gather x1, waiting for transfers between devices, local(): lax.all_gather(q_audio, 'seq', axis=0, tiled=True)  21.2 us
    dot_general x16, matrix products, audio_partial(): jnp.dot(queries, key_rows.T, preferred_element_type=jnp.float32) * factor  20.3 us
    dot_general x16, matrix products, video_head(): jnp.dot(weights, value_rows, preferred_element_type=jnp.float32)  17.1 us
    dot_general x16, matrix products, audio_partial(): jnp.dot(exponent.astype(jnp.bfloat16), value_rows, preferred_element_type...  14.9 us
    pmax x1, blocking collectives, local(): lax.pmax(block_peak.astype(jnp.bfloat16), 'seq').astype(block_peak.dtype)  13.6 us
    dynamic_update_slice x16, other arithmetic, local(): lax.map(video_head, (head_major(q_video, H), head_major(all_keys, H), hea...  10.5 us
    unnamed x7, local copies, waits for them, and re-layouts  6.98 us
  transfers between devices with their start and end apart: 5, of which 2 were waited for; matrix products, arithmetic and copies ran while one was open for 51% of the time, Pallas kernels for 0%

commit v1 on v0

v1 whole, which is shorter than its diff:
```python
import functools

import jax
import jax.numpy as jnp
from jax import lax
from jax.experimental import pallas as pl
from jax.experimental.pallas import tpu as pltpu
from jax.sharding import PartitionSpec as P

H = 16
EPS = 1e-06
LOG2E = 1.4426950408889634
BF16 = jnp.bfloat16
F32 = jnp.float32


def head_major(matrix, head_count):
    return matrix.reshape(matrix.shape[0], head_count, -1).transpose(1, 0, 2)


def settle(mixed):
    return mixed * lax.rsqrt(jnp.mean(mixed * mixed, axis=-1, keepdims=True) + EPS)


def video_head(triple):
    queries, key_rows, value_rows = triple
    factor = queries.shape[-1] ** (-0.5)
    scores = jnp.dot(queries, key_rows.T, preferred_element_type=F32) * factor
    row_peak = jnp.max(scores, axis=-1, keepdims=True)
    exponent = jnp.exp(scores - row_peak)
    weights = (exponent / jnp.sum(exponent, axis=-1, keepdims=True)).astype(BF16)
    return settle(jnp.dot(weights, value_rows, preferred_element_type=F32))


def audio_partial(triple):
    queries, key_rows, value_rows = triple
    factor = queries.shape[-1] ** (-0.5)
    scores = jnp.dot(queries, key_rows.T, preferred_element_type=F32) * factor
    block_peak = jnp.max(scores, axis=-1)
    exponent = jnp.exp(scores - block_peak[:, None])
    totals = jnp.sum(exponent, axis=-1)
    numerators = jnp.dot(exponent.astype(BF16), value_rows, preferred_element_type=F32)
    return (numerators, block_peak, totals)


def local_any(q_video, k_video, v_video, q_audio, k_audio, v_audio):
    all_queries, all_keys, all_values = (
        lax.all_gather(q_audio, "seq", axis=0, tiled=True),
        lax.all_gather(k_audio, "seq", axis=0, tiled=True),
        lax.all_gather(v_audio, "seq", axis=0, tiled=True),
    )
    video_rows = lax.map(
        video_head, (head_major(q_video, H), head_major(all_keys, H), head_major(all_values, H))
    )
    video_out = video_rows.transpose(1, 0, 2).reshape(q_video.shape[0], -1).astype(BF16)
    numerators, block_peak, totals = lax.map(
        audio_partial, (head_major(all_queries, H), head_major(k_video, H), head_major(v_video, H))
    )
    overall = lax.pmax(block_peak.astype(BF16), "seq").astype(block_peak.dtype)
    weight = jnp.exp(block_peak - overall)
    summed, denominator = (
        lax.psum_scatter(numerators * weight[..., None], "seq", scatter_dimension=1, tiled=True),
        lax.psum_scatter(totals * weight, "seq", scatter_dimension=1, tiled=True),
    )
    audio_mix = settle(summed / denominator[..., None])
    audio_out = audio_mix.transpose(1, 0, 2).reshape(audio_mix.shape[1], -1).astype(BF16)
    return (video_out, audio_out)


NT = (((1,), (1,)), ((), ()))


def attend(q, k, v, factor):
    s = lax.dot_general(q, k, NT, preferred_element_type=F32)
    m = jnp.max(s, axis=-1, keepdims=True)
    p = jnp.exp2((s - m) * factor).astype(BF16)
    ve = jnp.concatenate([v, jnp.ones_like(v)], axis=1)
    nd = jnp.dot(p, ve, preferred_element_type=F32)
    d = v.shape[1]
    return m * factor, nd[:, :d], nd[:, d:]


def kernel(
    heads,
    qv, kv, vv, qa, ka, va, vout, aout,
    q_all, k_all, v_all, qv_s, kv_s, vv_s, o_s, ao_s,
    nkeep, nsend, nrecv, msend, mrecv, l_own, l_recv, l_send, l_in,
    g_send, g_recv, p_send, p_recv, r_send, r_recv, loc,
):
    rows = qa.shape[0]
    width = qa.shape[1]
    dh = width // heads
    hw = width // 2
    hh = heads // 2
    keep = 4 * rows
    factor = dh ** (-0.5) * LOG2E

    me = lax.axis_index("seq")
    y, x, c = me // 4, (me // 2) % 2, me % 2

    def dev(yy, xx, cc):
        return {"seq": yy * 4 + xx * 2 + cc}

    X, Y, D, C = dev(y, 1 - x, c), dev(1 - y, x, c), dev(1 - y, 1 - x, c), dev(y, x, 1 - c)
    peers = (None, X, Y, D)

    barrier = pltpu.get_barrier_semaphore()
    for d in (X, Y, D, C):
        pl.semaphore_signal(barrier, inc=1, device_id=d, device_id_type=pl.DeviceIdType.MESH)

    locals_ = []

    def local_copy(src, dst):
        cp = pltpu.make_async_copy(src, dst, loc.at[len(locals_)])
        cp.start()
        locals_.append(cp)
        return cp

    ins = (qa, ka, va)
    alls = (q_all, k_all, v_all)
    c_own = [local_copy(a, b.at[pl.ds(0, rows)]) for a, b in zip(ins, alls)]
    c_kv = local_copy(kv, kv_s)
    c_vv = local_copy(vv, vv_s)
    c_qv = local_copy(qv, qv_s)

    l_own[...] = jnp.zeros_like(l_own)

    units = ((0, 0, 0), (0, 1, 1), (1, 0, 0), (2, 0, 1), (1, 1, 0), (2, 1, 1))

    def g(u, src_slot, dst_slot, to):
        a, h, _ = units[u]
        cols = pl.ds(h * hw, hw)
        if src_slot == 0:
            src = ins[a].at[:, cols]
        else:
            src = alls[a].at[pl.ds(src_slot * rows, rows), cols]
        return pltpu.make_async_remote_copy(
            src_ref=src,
            dst_ref=alls[a].at[pl.ds(dst_slot * rows, rows), cols],
            send_sem=g_send.at[u, dst_slot],
            recv_sem=g_recv.at[u, dst_slot],
            device_id=to,
            device_id_type=pl.DeviceIdType.MESH,
        )

    sent = {}
    started = []

    def go(u, src_slot, dst_slot, to):
        cp = g(u, src_slot, dst_slot, to)
        cp.start()
        sent[u, dst_slot] = cp
        started.append(cp)

    def own(u):
        go(u, 0, 1, X)
        go(u, 0, 2, Y)
        go(u, 0, 4, C)

    def forward_near(u):
        route = units[u][2]
        sent[u, 1].wait_recv()
        if route == 0:
            go(u, 1, 3, Y)
        go(u, 1, 5, C)
        sent[u, 2].wait_recv()
        if route == 1:
            go(u, 2, 3, X)
        go(u, 2, 6, C)

    def forward_far(u):
        sent[u, 3].wait_recv()
        go(u, 3, 7, C)

    def arrived(u):
        for s in (4, 5, 6, 7):
            sent[u, s].wait_recv()

    pl.semaphore_wait(barrier, 4)
    for u in range(6):
        own(u)
    forward_near(0)
    forward_near(1)
    forward_far(0)
    forward_far(1)
    c_own[0].wait()
    c_kv.wait()
    c_vv.wait()
    arrived(0)
    arrived(1)

    def lanes(h):
        return pl.ds(pl.multiple_of(h * dh, dh), dh)

    lane = lax.broadcasted_iota(jnp.int32, (2 * keep, dh), 1)

    def audio(half):
        def body(i, carry):
            for j in range(2):
                i2 = 2 * i + j
                at = lanes(half * hh + i2)
                m, n, d = attend(q_all[:, at], kv_s[:, at], vv_s[:, at], factor)
                n = n * (1.0 / d)
                l_own[half] = jnp.where(lane == i2, m + jnp.log2(d), l_own[half])
                nkeep[:, at] = n[:keep]
                nsend[:, at] = n[keep:].astype(BF16)
            return carry

        lax.fori_loop(0, hh // 2, body, 0)

    def exchange(half):
        cols = pl.ds(half * hw, hw)
        cps = []
        for i, (s, d) in enumerate((
            (nsend.at[:, cols], nrecv.at[:, cols]),
            (l_own.at[half, pl.ds(keep, keep)], l_recv.at[half]),
        )):
            cp = pltpu.make_async_remote_copy(
                src_ref=s, dst_ref=d, send_sem=p_send.at[half, i], recv_sem=p_recv.at[half, i],
                device_id=C, device_id_type=pl.DeviceIdType.MESH,
            )
            cp.start()
            started.append(cp)
            cps.append(cp)
        return cps

    def col(w, h, n):
        sel = lax.broadcasted_iota(jnp.int32, (n, dh), 1) == h
        return jnp.sum(jnp.where(sel, w, 0.0), axis=-1, keepdims=True)

    def merge(half, cps):
        for cp in cps:
            cp.wait_recv()
        l1, l2 = l_own[half, :keep], l_recv[half]
        top = jnp.maximum(l1, l2)
        a1, a2 = jnp.exp2(l1 - top), jnp.exp2(l2 - top)
        tot = a1 + a2
        inv = 1.0 / tot
        w1, w2 = a1 * inv, a2 * inv
        l_send[half] = top + jnp.log2(tot)
        for i in range(hh):
            at = pl.ds((half * hh + i) * dh, dh)
            n = nkeep[:, at] * w1[:, i : i + 1] + nrecv[:, at].astype(F32) * w2[:, i : i + 1]
            msend[:, at] = n.astype(BF16)
        cols = pl.ds(half * hw, hw)
        out = []
        for s in (3, 1, 2):
            r = pl.ds(s * rows, rows)
            for i, (src, dst) in enumerate((
                (msend.at[r, cols], mrecv.at[r, cols]),
                (l_send.at[half, r], l_in.at[half, r]),
            )):
                cp = pltpu.make_async_remote_copy(
                    src_ref=src, dst_ref=dst,
                    send_sem=r_send.at[half, s, i], recv_sem=r_recv.at[half, s, i],
                    device_id=peers[s], device_id_type=pl.DeviceIdType.MESH,
                )
                cp.start()
                started.append(cp)
                out.append(cp)
        return out

    def finish(half, cps):
        for cp in cps:
            cp.wait_recv()
        ls = [l_send[half, :rows]] + [l_in[half, s * rows : (s + 1) * rows] for s in (1, 2, 3)]
        top = functools.reduce(jnp.maximum, ls)
        es = [jnp.exp2(l - top) for l in ls]
        inv = 1.0 / functools.reduce(jnp.add, es)
        ws = [e * inv for e in es]
        for i in range(hh):
            at = pl.ds((half * hh + i) * dh, dh)
            n = msend[:rows, at].astype(F32) * ws[0][:, i : i + 1]
            for s in (1, 2, 3):
                n = n + mrecv[s * rows : (s + 1) * rows, at].astype(F32) * ws[s][:, i : i + 1]
            ao_s[:, at] = settle(n).astype(BF16)

    def video(half):
        def body(i, carry):
            for j in range(2):
                at = lanes(half * hh + 2 * i + j)
                _, n, d = attend(qv_s[:, at], k_all[:, at], v_all[:, at], factor)
                r = lax.rsqrt(jnp.mean(n * n, axis=-1, keepdims=True) + EPS * (d * d))
                o_s[:, at] = (n * r).astype(BF16)
            return carry

        lax.fori_loop(0, hh // 2, body, 0)
        cols = pl.ds(half * hw, hw)
        return local_copy(o_s.at[:, cols], vout.at[:, cols])

    audio(0)
    e0 = exchange(0)
    forward_near(2)
    forward_near(3)
    audio(1)
    e1 = exchange(1)
    forward_far(2)
    forward_far(3)
    m0 = merge(0, e0)
    m1 = merge(1, e1)
    forward_near(4)
    forward_near(5)
    c_own[1].wait()
    c_own[2].wait()
    c_qv.wait()
    arrived(2)
    arrived(3)
    v0 = video(0)
    forward_far(4)
    forward_far(5)
    arrived(4)
    arrived(5)
    v1 = video(1)
    finish(0, m0)
    finish(1, m1)
    ao = local_copy(ao_s, aout)
    for cp in (v0, v1, ao):
        cp.wait()
    for cp in started:
        cp.wait_send()


def local_one(q_video, k_video, v_video, q_audio, k_audio, v_audio):
    vr, width = q_video.shape
    rows = q_audio.shape[0]
    dh = width // H
    keep = 4 * rows
    any_ = pl.BlockSpec(memory_space=pl.ANY)
    dma = pltpu.SemaphoreType.DMA
    return pl.pallas_call(
        functools.partial(kernel, H),
        out_shape=(
            jax.ShapeDtypeStruct((vr, width), BF16),
            jax.ShapeDtypeStruct((rows, width), BF16),
        ),
        in_specs=[any_] * 6,
        out_specs=(any_, any_),
        scratch_shapes=[
            pltpu.VMEM((8 * rows, width), BF16),
            pltpu.VMEM((8 * rows, width), BF16),
            pltpu.VMEM((8 * rows, width), BF16),
            pltpu.VMEM((vr, width), BF16),
            pltpu.VMEM((vr, width), BF16),
            pltpu.VMEM((vr, width), BF16),
            pltpu.VMEM((vr, width), BF16),
            pltpu.VMEM((rows, width), BF16),
            pltpu.VMEM((keep, width), F32),
            pltpu.VMEM((keep, width), BF16),
            pltpu.VMEM((keep, width), BF16),
            pltpu.VMEM((keep, width), BF16),
            pltpu.VMEM((keep, width), BF16),
            pltpu.VMEM((2, 2 * keep, dh), F32),
            pltpu.VMEM((2, keep, dh), F32),
            pltpu.VMEM((2, keep, dh), F32),
            pltpu.VMEM((2, keep, dh), F32),
            dma((6, 8)),
            dma((6, 8)),
            dma((2, 2)),
            dma((2, 2)),
            dma((2, 4, 2)),
            dma((2, 4, 2)),
            dma((9,)),
        ],
        compiler_params=pltpu.CompilerParams(
            collective_id=0, has_side_effects=True, vmem_limit_bytes=48 * 1024 * 1024
        ),
    )(q_video, k_video, v_video, q_audio, k_audio, v_audio)


def solution(mesh):
    spec = P(("dp", "seq"), None)
    return jax.shard_map(
        local_one if mesh.shape["seq"] == 8 else local_any,
        mesh=mesh,
        in_specs=(spec,) * 6,
        out_specs=(spec, spec),
        check_vma=False,
    )
```

time: 183 us -> 46.8 us (0.26); the launches traced: 181 us -> 46.6 us
  waiting for transfers between devices: 56.9 us -> 0 us
  matrix products: 56.7 us -> 0 us
  Pallas kernels: 0 us -> 38.6 us
  other arithmetic: 21.9 us -> 0 us
  blocking collectives: 13.6 us -> 0 us
  between operations: 13.9 us -> 0.65 us
  local copies, waits for them, and re-layouts: 17 us -> 7.32 us
    dot_general x64 -> x0, matrix products: 56.7 us -> none  [the longest x16 20.3 us: audio_partial(): jnp.dot(queries, key_rows.T, preferred_element_type=jnp.float32) * factor]
    pallas_call x0 -> x1, Pallas kernels: none -> 38.6 us  [local_one(): pl.pallas_call(functools.partial(kernel, H), out_shape=(jax.ShapeDtypeStr...]
    reduce_scatter x1 -> x0, waiting for transfers between devices: 33.5 us -> none  [local(): lax.psum_scatter(numerators * weight[..., None], 'seq', scatter_dimension...]
    all_gather x3 -> x0, waiting for transfers between devices: 21.2 us -> none  [the longest x1 21.2 us: local(): lax.all_gather(q_audio, 'seq', axis=0, tiled=True)]
    pmax x1 -> x0, blocking collectives: 13.6 us -> none  [local(): lax.pmax(block_peak.astype(jnp.bfloat16), 'seq').astype(block_peak.dtype)]
    dynamic_update_slice x16 -> x0, other arithmetic: 10.5 us -> none  [local(): lax.map(video_head, (head_major(q_video, H), head_major(all_keys, H), hea...]
    all_gather x3 -> x0, local copies, waits for them, and re-layouts: 6.02 us -> none  [the longest x1 2.28 us: local(): lax.all_gather(q_audio, 'seq', axis=0, tiled=True)]
    reduce_sum x33 -> x0, other arithmetic: 5.96 us -> none  [the longest x16 3.27 us: audio_partial(): totals = jnp.sum(exponent, axis=-1)]
  transfers between devices with their start and end apart: 5 -> 0, of which waited for: 2 -> 0; matrix products, arithmetic and copies ran while one was open for 51% -> 0% of each run, Pallas kernels for 0% -> 0%
where the time goes in v1:
time: 46.8 us; the launch traced here: 46.6 us
  Pallas kernels  38.6 us (82%)
  local copies, waits for them, and re-layouts  7.32 us (16%)
  between operations  0.65 us (1%)
    pallas_call x1, Pallas kernels, local_one(): pl.pallas_call(functools.partial(kernel, H), out_shape=(jax.ShapeDtypeStr...  38.6 us
    unnamed x12, local copies, waits for them, and re-layouts  7.32 us

profile of v1, /device:TPU:0, one launch (start us, length us, event | category | flops | bytes accessed | tf_op | source)
XLA Modules:
  0.0 46.6 jit_solution(9796322854648720271)
XLA Ops:
  0.6 0.0 copy-start
  0.6 1.4 %copy-done = bf16[384,2048]{1,0:T(8,128)(2,1)S(1)} copy-done((bf16[384,2048]{1,0:T(8,128)(2,1)S(1)}, bf16[384,2048]{1,0:T(8,128)(2,1)}, u32[]{:S(2)}) %copy-start) | copy-done | bytes 1572888
  2.0 0.0 copy-start.1
  2.0 1.4 %copy-done.1 = bf16[384,2048]{1,0:T(8,128)(2,1)S(1)} copy-done((bf16[384,2048]{1,0:T(8,128)(2,1)S(1)}, bf16[384,2048]{1,0:T(8,128)(2,1)}, u32[]{:S(2)}) %copy-start.1) | copy-done | bytes 1572888
  3.4 0.0 copy-start.2
  3.5 0.9 %copy-done.2 = bf16[32,2048]{1,0:T(8,128)(2,1)S(1)} copy-done((bf16[32,2048]{1,0:T(8,128)(2,1)S(1)}, bf16[32,2048]{1,0:T(8,128)(2,1)}, u32[]{:S(2)}) %copy-start.2) | copy-done | bytes 131096
  4.4 0.0 copy-start.3
  4.4 0.9 %copy-done.3 = bf16[32,2048]{1,0:T(8,128)(2,1)S(1)} copy-done((bf16[32,2048]{1,0:T(8,128)(2,1)S(1)}, bf16[32,2048]{1,0:T(8,128)(2,1)}, u32[]{:S(2)}) %copy-start.3) | copy-done | bytes 131096
  5.3 0.0 copy-start.4
  5.3 0.9 %copy-done.4 = bf16[32,2048]{1,0:T(8,128)(2,1)S(1)} copy-done((bf16[32,2048]{1,0:T(8,128)(2,1)S(1)}, bf16[32,2048]{1,0:T(8,128)(2,1)}, u32[]{:S(2)}) %copy-start.4) | copy-done | bytes 131096
  6.2 38.6 %shard_map.77 = (bf16[384,2048]{1,0:T(8,128)(2,1)S(1)}, bf16[32,2048]{1,0:T(8,128)(2,1)S(1)}) custom-call(bf16[384,2048]{1,0:T(8,128)(2,1)S(1)} %copy-done, bf16[384,2048]{1,0:T(8,128)(2,1)S(1)} %copy-done.1, bf16[384,2048]{1,0:T(8,128)(2,1)} %vv.1, bf16[32,2048]{1,0:T(8,128)(2,1)S(1)} %copy-done.2, bf16[32,2048]{1,0:T(8,128)(2,1)S(1)} %copy-done.3, ...), custom_call_target="tpu_custom_call" | custom-call | tf_op jit(solution)/shard_map/pallas_call | solution.py:330
  44.8 1.1 %copy.10 = bf16[384,2048]{1,0:T(8,128)(2,1)} copy(bf16[384,2048]{1,0:T(8,128)(2,1)S(1)} %get-tuple-element.4) | data formatting | bytes 3145728
  46.0 0.7 %copy.11 = bf16[32,2048]{1,0:T(8,128)(2,1)} copy(bf16[32,2048]{1,0:T(8,128)(2,1)S(1)} %get-tuple-element.5) | data formatting | bytes 262144
Async XLA Ops:
  0.6 1.4 %copy-start = (bf16[384,2048]{1,0:T(8,128)(2,1)S(1)}, bf16[384,2048]{1,0:T(8,128)(2,1)}, u32[]{:S(2)}) copy-start(bf16[384,2048]{1,0:T(8,128)(2,1)} %qv.1) | copy-start | bytes 4718596
  2.0 1.4 %copy-start.1 = (bf16[384,2048]{1,0:T(8,128)(2,1)S(1)}, bf16[384,2048]{1,0:T(8,128)(2,1)}, u32[]{:S(2)}) copy-start(bf16[384,2048]{1,0:T(8,128)(2,1)} %kv.1) | copy-start | bytes 4718596
  3.4 0.9 %copy-start.2 = (bf16[32,2048]{1,0:T(8,128)(2,1)S(1)}, bf16[32,2048]{1,0:T(8,128)(2,1)}, u32[]{:S(2)}) copy-start(bf16[32,2048]{1,0:T(8,128)(2,1)} %qa.1) | copy-start | bytes 393220
  4.4 0.9 %copy-start.3 = (bf16[32,2048]{1,0:T(8,128)(2,1)S(1)}, bf16[32,2048]{1,0:T(8,128)(2,1)}, u32[]{:S(2)}) copy-start(bf16[32,2048]{1,0:T(8,128)(2,1)} %ka.1) | copy-start | bytes 393220
  5.3 0.9 %copy-start.4 = (bf16[32,2048]{1,0:T(8,128)(2,1)S(1)}, bf16[32,2048]{1,0:T(8,128)(2,1)}, u32[]{:S(2)}) copy-start(bf16[32,2048]{1,0:T(8,128)(2,1)} %va.1) | copy-start | bytes 393220

commit v2 on v1

--- a/solution.py
+++ b/solution.py
@@ -68,16 +68,15 @@
 
 
 NT = (((1,), (1,)), ((), ()))
+TN = (((0,), (0,)), ((), ()))
 
 
 def attend(q, k, v, factor):
-    s = lax.dot_general(q, k, NT, preferred_element_type=F32)
-    m = jnp.max(s, axis=-1, keepdims=True)
-    p = jnp.exp2((s - m) * factor).astype(BF16)
-    ve = jnp.concatenate([v, jnp.ones_like(v)], axis=1)
-    nd = jnp.dot(p, ve, preferred_element_type=F32)
-    d = v.shape[1]
-    return m * factor, nd[:, :d], nd[:, d:]
+    s = lax.dot_general(k, q, NT, preferred_element_type=F32)
+    m = jnp.max(s, axis=0, keepdims=True)
+    e = jnp.exp2((s - m) * factor)
+    n = lax.dot_general(e.astype(BF16), v, TN, preferred_element_type=F32)
+    return m * factor, n, jnp.sum(e, axis=0, keepdims=True)
 
 
 def kernel(
@@ -122,8 +121,6 @@
     c_kv = local_copy(kv, kv_s)
     c_vv = local_copy(vv, vv_s)
     c_qv = local_copy(qv, qv_s)
-
-    l_own[...] = jnp.zeros_like(l_own)
 
     units = ((0, 0, 0), (0, 1, 1), (1, 0, 0), (2, 0, 1), (1, 1, 0), (2, 1, 1))
 
@@ -156,15 +153,17 @@
         go(u, 0, 1, X)
         go(u, 0, 2, Y)
         go(u, 0, 4, C)
+        if u in (0, 1, 2, 3):
+            go(u, 0, 3, D)
 
     def forward_near(u):
         route = units[u][2]
         sent[u, 1].wait_recv()
-        if route == 0:
+        if route == 0 and u not in (0, 1, 2, 3):
             go(u, 1, 3, Y)
         go(u, 1, 5, C)
         sent[u, 2].wait_recv()
-        if route == 1:
+        if route == 1 and u not in (0, 1, 2, 3):
             go(u, 2, 3, X)
         go(u, 2, 6, C)
 
@@ -176,44 +175,31 @@
         for s in (4, 5, 6, 7):
             sent[u, s].wait_recv()
 
-    pl.semaphore_wait(barrier, 4)
-    for u in range(6):
-        own(u)
-    forward_near(0)
-    forward_near(1)
-    forward_far(0)
-    forward_far(1)
-    c_own[0].wait()
-    c_kv.wait()
-    c_vv.wait()
-    arrived(0)
-    arrived(1)
-
     def lanes(h):
         return pl.ds(pl.multiple_of(h * dh, dh), dh)
 
-    lane = lax.broadcasted_iota(jnp.int32, (2 * keep, dh), 1)
-
-    def audio(half):
+    def audio(first, last):
+        half = first // hh
+
         def body(i, carry):
-            for j in range(2):
-                i2 = 2 * i + j
-                at = lanes(half * hh + i2)
+            for j in range(4):
+                i2 = 4 * i + j - half * hh
+                at = lanes(4 * i + j)
                 m, n, d = attend(q_all[:, at], kv_s[:, at], vv_s[:, at], factor)
-                n = n * (1.0 / d)
-                l_own[half] = jnp.where(lane == i2, m + jnp.log2(d), l_own[half])
+                n = n * (1.0 / d).T
+                l_own[half, pl.ds(i2, 1)] = m + jnp.log2(d)
                 nkeep[:, at] = n[:keep]
                 nsend[:, at] = n[keep:].astype(BF16)
             return carry
 
-        lax.fori_loop(0, hh // 2, body, 0)
+        lax.fori_loop(first // 4, last // 4, body, 0)
 
     def exchange(half):
         cols = pl.ds(half * hw, hw)
         cps = []
         for i, (s, d) in enumerate((
             (nsend.at[:, cols], nrecv.at[:, cols]),
-            (l_own.at[half, pl.ds(keep, keep)], l_recv.at[half]),
+            (l_own.at[half, :, pl.ds(keep, keep)], l_recv.at[half]),
         )):
             cp = pltpu.make_async_remote_copy(
                 src_ref=s, dst_ref=d, send_sem=p_send.at[half, i], recv_sem=p_recv.at[half, i],
@@ -224,19 +210,15 @@
             cps.append(cp)
         return cps
 
-    def col(w, h, n):
-        sel = lax.broadcasted_iota(jnp.int32, (n, dh), 1) == h
-        return jnp.sum(jnp.where(sel, w, 0.0), axis=-1, keepdims=True)
-
     def merge(half, cps):
         for cp in cps:
             cp.wait_recv()
-        l1, l2 = l_own[half, :keep], l_recv[half]
+        l1, l2 = l_own[half, :, :keep], l_recv[half]
         top = jnp.maximum(l1, l2)
         a1, a2 = jnp.exp2(l1 - top), jnp.exp2(l2 - top)
         tot = a1 + a2
         inv = 1.0 / tot
-        w1, w2 = a1 * inv, a2 * inv
+        w1, w2 = (a1 * inv).T, (a2 * inv).T
         l_send[half] = top + jnp.log2(tot)
         for i in range(hh):
             at = pl.ds((half * hh + i) * dh, dh)
@@ -248,7 +230,7 @@
             r = pl.ds(s * rows, rows)
             for i, (src, dst) in enumerate((
                 (msend.at[r, cols], mrecv.at[r, cols]),
-                (l_send.at[half, r], l_in.at[half, r]),
+                (l_send.at[half], l_in.at[half, s]),
             )):
                 cp = pltpu.make_async_remote_copy(
                     src_ref=src, dst_ref=dst,
@@ -263,7 +245,7 @@
     def finish(half, cps):
         for cp in cps:
             cp.wait_recv()
-        ls = [l_send[half, :rows]] + [l_in[half, s * rows : (s + 1) * rows] for s in (1, 2, 3)]
+        ls = [l_send[half].T[:rows]] + [l_in[half, s].T[s * rows : (s + 1) * rows] for s in (1, 2, 3)]
         top = functools.reduce(jnp.maximum, ls)
         es = [jnp.exp2(l - top) for l in ls]
         inv = 1.0 / functools.reduce(jnp.add, es)
@@ -275,49 +257,100 @@
                 n = n + mrecv[s * rows : (s + 1) * rows, at].astype(F32) * ws[s][:, i : i + 1]
             ao_s[:, at] = settle(n).astype(BF16)
 
-    def video(half):
+    def video(first, last):
         def body(i, carry):
-            for j in range(2):
-                at = lanes(half * hh + 2 * i + j)
+            for j in range(4):
+                at = lanes(4 * i + j)
                 _, n, d = attend(qv_s[:, at], k_all[:, at], v_all[:, at], factor)
-                r = lax.rsqrt(jnp.mean(n * n, axis=-1, keepdims=True) + EPS * (d * d))
+                r = lax.rsqrt(jnp.mean(n * n, axis=-1, keepdims=True) + (EPS * (d * d)).T)
                 o_s[:, at] = (n * r).astype(BF16)
             return carry
 
-        lax.fori_loop(0, hh // 2, body, 0)
-        cols = pl.ds(half * hw, hw)
+        lax.fori_loop(first // 4, last // 4, body, 0)
+        cols = pl.ds(first * dh, (last - first) * dh)
         return local_copy(o_s.at[:, cols], vout.at[:, cols])
 
-    audio(0)
+    q4 = hh // 2
+    pl.semaphore_wait(barrier, 4)
+    own(0)
+    own(1)
+    forward_near(0)
+    forward_near(1)
+    own(2)
+    own(3)
+    forward_far(0)
+    forward_far(1)
+    c_own[0].wait()
+    c_kv.wait()
+    c_vv.wait()
+    arrived(0)
+    arrived(1)
+    audio(0, hh)
     e0 = exchange(0)
+    own(4)
+    own(5)
     forward_near(2)
     forward_near(3)
-    audio(1)
+    audio(hh, heads)
     e1 = exchange(1)
     forward_far(2)
     forward_far(3)
     m0 = merge(0, e0)
-    m1 = merge(1, e1)
     forward_near(4)
     forward_near(5)
+    m1 = merge(1, e1)
     c_own[1].wait()
     c_own[2].wait()
     c_qv.wait()
     arrived(2)
     arrived(3)
-    v0 = video(0)
+    v0 = video(0, hh)
     forward_far(4)
     forward_far(5)
+    finish(0, m0)
     arrived(4)
     arrived(5)
-    v1 = video(1)
-    finish(0, m0)
+    v1 = video(hh, heads)
     finish(1, m1)
     ao = local_copy(ao_s, aout)
     for cp in (v0, v1, ao):
         cp.wait()
     for cp in started:
         cp.wait_send()
+
+
+def land_kernel(v, a, vout, aout, vbuf, abuf, s_in, s_out, *, pieces):
+    step = v.shape[0] // pieces
+    pairs = [(a, abuf, aout)]
+    for i in range(pieces):
+        r = pl.ds(i * step, step)
+        pairs.append((v.at[r], vbuf.at[r], vout.at[r]))
+    ins = [pltpu.make_async_copy(p[0], p[1], s_in.at[i]) for i, p in enumerate(pairs)]
+    outs = [pltpu.make_async_copy(p[1], p[2], s_out.at[i]) for i, p in enumerate(pairs)]
+    for cp in ins:
+        cp.start()
+    for i, cp in enumerate(ins):
+        cp.wait()
+        outs[i].start()
+    for cp in outs:
+        cp.wait()
+
+
+def land(v, a, pieces=6):
+    any_ = pl.BlockSpec(memory_space=pl.ANY)
+    return pl.pallas_call(
+        functools.partial(land_kernel, pieces=pieces),
+        out_shape=(jax.ShapeDtypeStruct(v.shape, v.dtype), jax.ShapeDtypeStruct(a.shape, a.dtype)),
+        in_specs=[any_] * 2,
+        out_specs=(any_, any_),
+        scratch_shapes=[
+            pltpu.VMEM(v.shape, v.dtype),
+            pltpu.VMEM(a.shape, a.dtype),
+            pltpu.SemaphoreType.DMA((pieces + 1,)),
+            pltpu.SemaphoreType.DMA((pieces + 1,)),
+        ],
+        compiler_params=pltpu.CompilerParams(vmem_limit_bytes=63 * 1024 * 1024),
+    )(v, a)
 
 
 def local_one(q_video, k_video, v_video, q_audio, k_audio, v_audio):
@@ -327,7 +360,7 @@
     keep = 4 * rows
     any_ = pl.BlockSpec(memory_space=pl.ANY)
     dma = pltpu.SemaphoreType.DMA
-    return pl.pallas_call(
+    return land(*pl.pallas_call(
         functools.partial(kernel, H),
         out_shape=(
             jax.ShapeDtypeStruct((vr, width), BF16),
@@ -349,22 +382,22 @@
             pltpu.VMEM((keep, width), BF16),
             pltpu.VMEM((keep, width), BF16),
             pltpu.VMEM((keep, width), BF16),
-            pltpu.VMEM((2, 2 * keep, dh), F32),
-            pltpu.VMEM((2, keep, dh), F32),
-            pltpu.VMEM((2, keep, dh), F32),
-            pltpu.VMEM((2, keep, dh), F32),
+            pltpu.VMEM((2, H // 2, 2 * keep), F32),
+            pltpu.VMEM((2, H // 2, keep), F32),
+            pltpu.VMEM((2, H // 2, keep), F32),
+            pltpu.VMEM((2, 4, H // 2, keep), F32),
             dma((6, 8)),
             dma((6, 8)),
             dma((2, 2)),
             dma((2, 2)),
             dma((2, 4, 2)),
             dma((2, 4, 2)),
-            dma((9,)),
+            dma((11,)),
         ],
         compiler_params=pltpu.CompilerParams(
-            collective_id=0, has_side_effects=True, vmem_limit_bytes=48 * 1024 * 1024
+            collective_id=0, has_side_effects=True, vmem_limit_bytes=63 * 1024 * 1024
         ),
-    )(q_video, k_video, v_video, q_audio, k_audio, v_audio)
+    )(q_video, k_video, v_video, q_audio, k_audio, v_audio))
 
 
 def solution(mesh):

time: 46.8 us -> 37.1 us (0.79)
  local copies, waits for them, and re-layouts: 7.32 us -> 0 us
  Pallas kernels: 38.6 us -> 36.3 us
    unnamed x12 -> x0, local copies, waits for them, and re-layouts: 7.32 us -> none
    pallas_call x1, Pallas kernels: 38.6 us -> 34.1 us  [local_one(): pl.pallas_call(functools.partial(kernel, H), out_shape=(jax.ShapeDtypeStr...]
    pallas_call x0 -> x1, Pallas kernels: none -> 2.28 us  [land(): pl.pallas_call(functools.partial(land_kernel, pieces=pieces), out_shape=(...]
where the time goes in v2:
time: 37.1 us; the launch traced here: 37 us
  Pallas kernels  36.3 us (98%)
  between operations  0.64 us (2%)
    pallas_call x1, Pallas kernels, local_one(): pl.pallas_call(functools.partial(kernel, H), out_shape=(jax.ShapeDtypeStr...  34.1 us
    pallas_call x1, Pallas kernels, land(): pl.pallas_call(functools.partial(land_kernel, pieces=pieces), out_shape=(...  2.28 us

profile of v2, /device:TPU:0, one launch (start us, length us, event | category | flops | bytes accessed | tf_op | source)
XLA Modules:
  0.0 37.0 jit_solution(9948960147874197128)
XLA Ops:
  0.6 34.1 %shard_map.77 = (bf16[384,2048]{1,0:T(8,128)(2,1)}, bf16[32,2048]{1,0:T(8,128)(2,1)}) custom-call(bf16[384,2048]{1,0:T(8,128)(2,1)} %qv.1, bf16[384,2048]{1,0:T(8,128)(2,1)} %kv.1, bf16[384,2048]{1,0:T(8,128)(2,1)} %vv.1, bf16[32,2048]{1,0:T(8,128)(2,1)} %qa.1, bf16[32,2048]{1,0:T(8,128)(2,1)} %ka.1, bf16[32,2048]{1,0:T(8,128)(2,1)} %va.1), custom_call_target="tpu_custom_call" | custom-call | tf_op jit(solution)/shard_map/pallas_call | solution.py:363
  34.7 2.3 %shard_map.78 = (bf16[384,2048]{1,0:T(8,128)(2,1)}, bf16[32,2048]{1,0:T(8,128)(2,1)}) custom-call(bf16[384,2048]{1,0:T(8,128)(2,1)} %get-tuple-element.4.v, bf16[32,2048]{1,0:T(8,128)(2,1)} %get-tuple-element.5.a), custom_call_target="tpu_custom_call" | custom-call | tf_op jit(solution)/shard_map/pallas_call | solution.py:341

commit v3 on v2

--- a/solution.py
+++ b/solution.py
@@ -298,13 +298,13 @@
     m0 = merge(0, e0)
     forward_near(4)
     forward_near(5)
-    m1 = merge(1, e1)
     c_own[1].wait()
     c_own[2].wait()
     c_qv.wait()
     arrived(2)
     arrived(3)
     v0 = video(0, hh)
+    m1 = merge(1, e1)
     forward_far(4)
     forward_far(5)
     finish(0, m0)

time: 37.1 us -> 36.4 us (0.981)
  Pallas kernels: 36.3 us -> 35.6 us
    pallas_call x1, Pallas kernels: 34.1 us -> 33.3 us  [local_one(): pl.pallas_call(functools.partial(kernel, H), out_shape=(jax.ShapeDtypeStr...]
where the time goes in v3:
time: 36.4 us; the launch traced here: 36.2 us
  Pallas kernels  35.6 us (98%)
  between operations  0.64 us (2%)
    pallas_call x1, Pallas kernels, local_one(): pl.pallas_call(functools.partial(kernel, H), out_shape=(jax.ShapeDtypeStr...  33.3 us
    pallas_call x1, Pallas kernels, land(): pl.pallas_call(functools.partial(land_kernel, pieces=pieces), out_shape=(...  2.28 us

profile of v3, /device:TPU:0, one launch (start us, length us, event | category | flops | bytes accessed | tf_op | source)
XLA Modules:
  0.0 36.2 jit_solution(7922159139954393130)
XLA Ops:
  0.6 33.3 %shard_map.77 = (bf16[384,2048]{1,0:T(8,128)(2,1)}, bf16[32,2048]{1,0:T(8,128)(2,1)}) custom-call(bf16[384,2048]{1,0:T(8,128)(2,1)} %qv.1, bf16[384,2048]{1,0:T(8,128)(2,1)} %kv.1, bf16[384,2048]{1,0:T(8,128)(2,1)} %vv.1, bf16[32,2048]{1,0:T(8,128)(2,1)} %qa.1, bf16[32,2048]{1,0:T(8,128)(2,1)} %ka.1, bf16[32,2048]{1,0:T(8,128)(2,1)} %va.1), custom_call_target="tpu_custom_call" | custom-call | tf_op jit(solution)/shard_map/pallas_call | solution.py:363
  34.0 2.3 %shard_map.78 = (bf16[384,2048]{1,0:T(8,128)(2,1)}, bf16[32,2048]{1,0:T(8,128)(2,1)}) custom-call(bf16[384,2048]{1,0:T(8,128)(2,1)} %get-tuple-element.4.v, bf16[32,2048]{1,0:T(8,128)(2,1)} %get-tuple-element.5.a), custom_call_target="tpu_custom_call" | custom-call | tf_op jit(solution)/shard_map/pallas_call | solution.py:341
